TPU v7x, 512 devices: a whole 4x8x8 slice. The times are simulated.
512 devices in a mesh: ctx: 128 (over z, y, core), head: 4 (over x).
Axes of the slice: x: 4, y: 8, z: 8, core: 2. Of those that a mesh axis runs over, the one named last changes fastest.
Arguments:
- queries: bfloat16 [32768, 2048], P('ctx', 'head'), may hold values from -0.4375 to 0.4375
- keys: bfloat16 [32768, 2048], P('ctx', 'head'), may hold values from -0.4375 to 0.4375
- values: bfloat16 [32768, 2048], P('ctx', 'head'), may hold values from -0.4375 to 0.4375
- out_grad: bfloat16 [32768, 2048], P('ctx', 'head'), may hold values from -0.4375 to 0.4375
Outputs:
- query_grad: bfloat16 [32768, 2048], P('ctx', 'head')
- key_grad: bfloat16 [32768, 2048], P('ctx', 'head')
- value_grad: bfloat16 [32768, 2048], P('ctx', 'head')
All inputs are finite; a program needn't handle non-finite values.
Results may differ from a plain program's by a relative error of at most 0.0049.
Values sent between devices are 32-bit elements; how exact they have to be, the bound alone decides.
No kernel may reach another device: no remote copies, remote signals or barrier semaphores. Data moves between devices by JAX's collectives and lax.ppermute only.
A program may use at most 128 MiB of HBM per device.

v0:
```python
import jax
import jax.numpy as jnp
from jax import lax
from jax.sharding import PartitionSpec as P

DH = 64


def carried_in(value, axis, join, neutral, backward):
    count, mine = (lax.axis_size(axis), lax.axis_index(axis))
    pieces = lax.all_gather(value, axis)
    if backward:
        pieces = pieces[::-1]
        mine = count - 1 - mine
    running = jnp.full_like(value, 0) + jnp.asarray(neutral, value.dtype)

    def turn(position, running):
        longer = join(running, pieces[position])
        return jnp.where(position < mine, longer, running)

    return lax.fori_loop(0, count - 1, turn, running)


def add_states(earlier, later):
    return jax.tree.map(lambda first, second: first + second, earlier, later)


def body(queries, keys, values, out_grad):
    length = queries.shape[0]
    width = queries.shape[1]
    local_heads = width // DH
    q = queries.reshape(length, local_heads, DH)
    k = keys.reshape(length, local_heads, DH)
    v = values.reshape(length, local_heads, DH)
    d = out_grad.reshape(length, local_heads, DH)
    kv = jnp.einsum("thd,the->hde", k, v, preferred_element_type=jnp.float32).reshape(
        local_heads, DH * DH
    )
    g = jnp.einsum("thd,the->hde", q, d, preferred_element_type=jnp.float32).reshape(
        local_heads, DH * DH
    )
    zeros = jnp.zeros_like(kv)
    prefix = carried_in(kv, "ctx", add_states, zeros, False)
    suffix = carried_in(g, "ctx", add_states, zeros, True)
    rows = lax.broadcasted_iota(jnp.int32, (length, length), 0)
    cols = lax.broadcasted_iota(jnp.int32, (length, length), 1)
    keep = rows >= cols
    a_score = jnp.einsum("thd,shd->hts", q, k, preferred_element_type=jnp.float32)
    b_score = jnp.einsum("the,she->hts", d, v, preferred_element_type=jnp.float32)
    a_score = jnp.where(keep[None], a_score, 0.0).astype(jnp.bfloat16)
    b_score = jnp.where(keep[None], b_score, 0.0).astype(jnp.bfloat16)
    prefix_r = prefix.astype(jnp.bfloat16).reshape(local_heads, DH, DH)
    suffix_r = suffix.astype(jnp.bfloat16).reshape(local_heads, DH, DH)
    dq = jnp.einsum("hts,shd->thd", b_score, k, preferred_element_type=jnp.float32)
    dq = dq + jnp.einsum("the,hde->thd", d, prefix_r, preferred_element_type=jnp.float32)
    dk = jnp.einsum("hts,thd->shd", b_score, q, preferred_element_type=jnp.float32)
    dk = dk + jnp.einsum("she,hde->shd", v, suffix_r, preferred_element_type=jnp.float32)
    dv = jnp.einsum("hts,the->she", a_score, d, preferred_element_type=jnp.float32)
    dv = dv + jnp.einsum("shd,hde->she", k, suffix_r, preferred_element_type=jnp.float32)
    query_grad = dq.astype(jnp.bfloat16).reshape(length, width)
    key_grad = dk.astype(jnp.bfloat16).reshape(length, width)
    value_grad = dv.astype(jnp.bfloat16).reshape(length, width)
    return (query_grad, key_grad, value_grad)


def solution(mesh):
    placed = (P("ctx", "head"), P("ctx", "head"), P("ctx", "head"), P("ctx", "head"))
    return jax.shard_map(
        body,
        mesh=mesh,
        in_specs=placed,
        out_specs=(P("ctx", "head"), P("ctx", "head"), P("ctx", "head")),
        check_vma=False,
    )
```

profile of v0, /device:TPU:1, one launch (start us, length us, event | category | flops | bytes accessed | tf_op | source)
XLA Modules:
  0.0 388.4 jit_solution(9298369829042499991)
XLA Ops:
  7.2 1.1 copy.31
  8.4 1.1 copy.34
  12.4 105.8 %all-gather.5.cloned.1.call-done = f32[128,8,4096]{2,1,0:T(8,128)} async-done(((f32[1,8,4096]{2,1,0:T(8,128)}), f32[128,8,4096]{2,1,0:T(8,128)}) %all-gather.5.cloned.1.call-update) | async-done | bytes 16777232 | tf_op jit(solution)/shard_map/all_gather | solution.py:11
  118.2 11.6 %rev.3 = f32[128,8,4096]{2,1,0:T(8,128)} reverse(f32[128,8,4096]{2,1,0:T(8,128)} %all-gather.5.cloned.1.call-done), dimensions={0} | reverse | bytes 33554432 | tf_op jit(solution)/shard_map/rev | solution.py:13
  129.7 123.6 %while.29 = (s32[]{:T(128)}, f32[8,4096]{1,0:T(8,128)S(1)}, s32[]{:T(128)}, f32[128,8,4096]{2,1,0:T(8,128)}, s32[]{:T(128)}, /*index=5*/s32[]{:T(128)}) while((s32[]{:T(128)}, f32[8,4096]{1,0:T(8,128)S(1)}, s32[]{:T(128)}, f32[128,8,4096]{2,1,0:T(8,128)}, s32[]{:T(128)}, /*index=5*/s32[]{:T(128)}) %tuple.69), condition=%wide.region_3.4_spmd.clone, body=%wide.region_2.3_spmd.clone.sunk | while | flops 98308 | bytes 393309 | solution.py:21
  133.6 1.0 add_select_fusion.5
  134.6 1.0 add_select_fusion.5
  140.4 1.0 add_select_fusion.5
  144.3 1.0 add_select_fusion.5
  147.2 1.0 add_select_fusion.5
  150.1 1.0 add_select_fusion.5
  153.0 0.9 add_select_fusion.5
  155.0 0.9 add_select_fusion.5
  155.9 1.0 add_select_fusion.5
  156.9 0.9 add_select_fusion.5
  157.9 0.9 add_select_fusion.5
  158.9 0.9 add_select_fusion.5
  159.8 0.9 add_select_fusion.5
  160.8 0.9 add_select_fusion.5
  161.8 0.9 add_select_fusion.5
  162.7 0.9 add_select_fusion.5
  163.7 0.9 add_select_fusion.5
  164.7 0.9 add_select_fusion.5
  165.6 0.9 add_select_fusion.5
  166.6 0.9 add_select_fusion.5
  167.6 0.9 add_select_fusion.5
  168.6 0.9 add_select_fusion.5
  169.5 0.9 add_select_fusion.5
  170.5 0.9 add_select_fusion.5
  171.5 0.9 add_select_fusion.5
  172.4 0.9 add_select_fusion.5
  173.4 0.9 add_select_fusion.5
  174.4 1.0 add_select_fusion.5
  181.2 0.9 add_select_fusion.5
  182.2 1.0 add_select_fusion.5
  185.1 1.0 add_select_fusion.5
  186.1 1.0 add_select_fusion.5
  188.1 1.0 add_select_fusion.5
  189.0 1.0 add_select_fusion.5
  191.1 1.0 add_select_fusion.5
  192.0 1.0 add_select_fusion.5
  193.0 0.9 add_select_fusion.5
  194.0 0.9 add_select_fusion.5
  194.9 1.0 add_select_fusion.5
  195.9 0.9 add_select_fusion.5
  197.9 1.0 add_select_fusion.5
  198.8 1.0 add_select_fusion.5
  200.8 1.0 add_select_fusion.5
  201.8 1.0 add_select_fusion.5
  203.8 0.9 add_select_fusion.5
  204.7 1.0 add_select_fusion.5
  207.7 1.0 add_select_fusion.5
  208.6 1.0 add_select_fusion.5
  210.6 1.0 add_select_fusion.5
  211.6 1.0 add_select_fusion.5
  212.6 0.9 add_select_fusion.5
  213.6 0.9 add_select_fusion.5
  218.4 1.0 add_select_fusion.5
  219.4 0.9 add_select_fusion.5
  220.4 0.9 add_select_fusion.5
  221.3 0.9 add_select_fusion.5
  222.3 0.9 add_select_fusion.5
  223.3 0.9 add_select_fusion.5
  255.5 123.1 %while.28 = (s32[]{:T(128)}, f32[8,4096]{1,0:T(8,128)S(1)}, s32[]{:T(128)}, f32[128,8,4096]{2,1,0:T(8,128)}, s32[]{:T(128)}, /*index=5*/s32[]{:T(128)}) while((s32[]{:T(128)}, f32[8,4096]{1,0:T(8,128)S(1)}, s32[]{:T(128)}, f32[128,8,4096]{2,1,0:T(8,128)}, s32[]{:T(128)}, /*index=5*/s32[]{:T(128)}) %tuple.66), condition=%wide.region_1.2_spmd.clone, body=%wide.region_0.1_spmd.clone.sunk | while | flops 98308 | bytes 393309 | solution.py:21
  (228 shorter events, 193.4 us)
Async XLA Ops:
  7.2 3.4 copy-start
  7.2 3.5 copy-start.1
  7.2 111.0 %all-gather.5.cloned.1.call-start = ((), (), s32[]{:S(2)}) async-start(), calls=%async_computation.1 | async-start | bytes 16908288 | tf_op jit(solution)/shard_map/all_gather | solution.py:11
  10.5 245.1 %all-gather.3.cloned.1.call-start = ((), (), s32[]{:S(2)}) async-start(), calls=%async_computation | async-start | bytes 16908288 | tf_op jit(solution)/shard_map/all_gather | solution.py:11
Sparse Core Ops, SparseCore 0:
  11.7 106.3 all-gather.4
  121.9 98.4 all-gather.2
where the time goes:
time: 393 us; the launch traced here: 388 us
  other arithmetic  241 us (61%)
  waiting for transfers between devices  106 us (27%)
  local copies, waits for them, and re-layouts  18.5 us (5%)
  between operations  14.2 us (4%)
  loops' own time  5.79 us (1%)
    select_n x254, other arithmetic, turn(): return jnp.where(position < mine, longer, running)  241 us
    all_gather x2, waiting for transfers between devices, carried_in(): pieces = lax.all_gather(value, axis)  106 us
    rev x1, local copies, waits for them, and re-layouts, carried_in(): pieces = pieces[::-1]  11.6 us
  transfers between devices with their start and end apart: 2, of which 1 were waited for; matrix products, arithmetic and copies ran while one was open for 35% of the time, Pallas kernels for 0%

commit v1 on v0

v1 whole, which is shorter than its diff:
```python
import functools

import jax
import jax.numpy as jnp
from jax import lax
from jax.experimental import pallas as pl
from jax.experimental.pallas import tpu as pltpu
from jax.sharding import PartitionSpec as P

DH = 64
PAIR = 2 * DH
QUAD = 4 * DH
VMEM = pltpu.VMEM
F32 = jnp.float32
BF16 = jnp.bfloat16
NT = (((1,), (1,)), ((), ()))
NN = (((1,), (0,)), ((), ()))
TN = (((0,), (0,)), ((), ()))


def dot(a, b, dims):
    return lax.dot_general(a, b, dims, preferred_element_type=F32)


def low_lanes(shape):
    return (lax.broadcasted_iota(jnp.int32, shape, 1) & DH) == 0


def in_block(q_ref, k_ref, v_ref, d_ref, dq_ref, dk_ref, dv_ref):
    length, width = q_ref.shape
    rows = lax.broadcasted_iota(jnp.int32, (length, length), 0)
    cols = lax.broadcasted_iota(jnp.int32, (length, length), 1)
    keep = rows >= cols
    keep_t = cols >= rows
    low = low_lanes((length, PAIR))
    for p in range(width // PAIR):
        at = pl.ds(p * PAIR, PAIR)
        q, k, v, d = q_ref[:, at], k_ref[:, at], v_ref[:, at], d_ref[:, at]
        dq = dk = dv = 0.0
        for mine in (low, ~low):
            kh = jnp.where(mine, k, 0)
            vh = jnp.where(mine, v, 0)
            qh = jnp.where(mine, q, 0)
            dh = jnp.where(mine, d, 0)
            b = jnp.where(keep, dot(d, vh, NT), 0.0).astype(BF16)
            bt = jnp.where(keep_t, dot(v, dh, NT), 0.0).astype(BF16)
            at_ = jnp.where(keep_t, dot(k, qh, NT), 0.0).astype(BF16)
            dq += dot(b, kh, NN)
            dk += dot(bt, qh, NN)
            dv += dot(at_, dh, NN)
        dq_ref[:, at] = dq
        dk_ref[:, at] = dk
        dv_ref[:, at] = dv


def packed_state(a_ref, b_ref, out_ref, base):
    width = a_ref.shape[1]
    low = low_lanes((DH, PAIR))
    for g in range(width // QUAD):
        at = pl.ds(g * QUAD, QUAD)
        full = dot(a_ref[:, at], b_ref[:, at], TN)
        for j in range(2):
            lanes = slice(j * PAIR, (j + 1) * PAIR)
            top = full[j * PAIR : j * PAIR + DH, lanes]
            bottom = full[j * PAIR + DH : (j + 1) * PAIR, lanes]
            out_ref[pl.ds(base + (2 * g + j) * DH, DH), :] = jnp.where(low, top, bottom)


def states_kernel(early, q_ref, k_ref, v_ref, d_ref, state_ref, dq_ref, dk_ref, dv_ref):
    half = state_ref.shape[0] // 2
    packed_state(k_ref, v_ref, state_ref, 0)
    packed_state(q_ref, d_ref, state_ref, half)

    @pl.when(lax.axis_index("ctx") < early)
    def _():
        in_block(q_ref, k_ref, v_ref, d_ref, dq_ref, dk_ref, dv_ref)


def chip_sum_kernel(both_ref, sum_ref):
    half = sum_ref.shape[0]
    core = lax.axis_index("ctx") % 2
    at = pl.ds(pl.multiple_of(core * half, half), half)
    sum_ref[...] = both_ref[0, at, :] + both_ref[1, at, :]


def scan_kernel(chips, lead, part_ref, out_ref):
    rows = part_ref.shape[0]
    each = rows // chips
    core = lax.axis_index("ctx") % 2
    r = lax.broadcasted_iota(jnp.int32, (rows, rows), 0)
    c = lax.broadcasted_iota(jnp.int32, (rows, rows), 1)
    ahead = (r // each + lead) % chips - (c // each + lead) % chips
    ahead = jnp.where(core == 0, ahead, -ahead)
    take = jnp.where((ahead > 0) & (r % each == c % each), 1.0, 0.0).astype(BF16)
    x = part_ref[...]
    high = x.astype(BF16)
    rest = x - high.astype(F32)
    middle = rest.astype(BF16)
    low = (rest - middle.astype(F32)).astype(BF16)
    out_ref[...] = (dot(take, low, NN) + dot(take, middle, NN)) + dot(take, high, NN)


def block_diagonal(packed, g):
    low = low_lanes((DH, PAIR))
    zero = jnp.zeros((PAIR, PAIR), BF16)
    blocks = []
    for j in range(2):
        two = packed[(2 * g + j) * DH : (2 * g + j + 1) * DH]
        blocks.append(
            jnp.concatenate([jnp.where(low, two, 0.0), jnp.where(low, 0.0, two)], axis=0).astype(BF16)
        )
    return jnp.concatenate(
        [
            jnp.concatenate([blocks[0], zero], axis=1),
            jnp.concatenate([zero, blocks[1]], axis=1),
        ],
        axis=0,
    )


def final_kernel(
    early, q_ref, k_ref, v_ref, d_ref, state_ref, carry_ref, iq_ref, ik_ref, iv_ref,
    oq_ref, ok_ref, ov_ref, dq_ref, dk_ref, dv_ref,
):
    half = carry_ref.shape[1]
    width = q_ref.shape[1]
    me = lax.axis_index("ctx")
    core = me % 2

    def finish(sq_ref, sk_ref, sv_ref):
        prefix = carry_ref[0] + jnp.where(core == 1, state_ref[0, :half, :], 0.0)
        suffix = carry_ref[1] + jnp.where(core == 0, state_ref[1, half:, :], 0.0)
        for g in range(width // QUAD):
            at = pl.ds(g * QUAD, QUAD)
            pre, suf = block_diagonal(prefix, g), block_diagonal(suffix, g)
            oq_ref[:, at] = (sq_ref[:, at] + dot(d_ref[:, at], pre, NT)).astype(BF16)
            ok_ref[:, at] = (sk_ref[:, at] + dot(v_ref[:, at], suf, NT)).astype(BF16)
            ov_ref[:, at] = (sv_ref[:, at] + dot(k_ref[:, at], suf, NN)).astype(BF16)

    @pl.when(me < early)
    def _():
        finish(iq_ref, ik_ref, iv_ref)

    @pl.when(me >= early)
    def _():
        in_block(q_ref, k_ref, v_ref, d_ref, dq_ref, dk_ref, dv_ref)
        finish(dq_ref, dk_ref, dv_ref)


def call(kernel, outs, n_in, scratch=(), out_space=VMEM):
    return pl.pallas_call(
        kernel,
        out_shape=outs,
        in_specs=[pl.BlockSpec(memory_space=VMEM)] * n_in,
        out_specs=jax.tree.map(lambda _: pl.BlockSpec(memory_space=out_space), outs),
        scratch_shapes=scratch,
        compiler_params=pltpu.CompilerParams(vmem_limit_bytes=24 * 1024 * 1024),
    )


def body(queries, keys, values, out_grad):
    length, width = queries.shape
    half = width // 2
    count = lax.axis_size("ctx")
    chips = count // 2
    early = count // 2
    lead = chips // 2 + 4
    order = [(s + lead) % chips for s in range(chips)]
    pairs = [[2 * c, 2 * c + 1] for c in range(chips)]
    across = [[2 * c + core for c in order] for core in range(2)]

    wide = jax.ShapeDtypeStruct((length, width), F32)
    state_shape = jax.ShapeDtypeStruct((2 * half, PAIR), F32)
    half_shape = jax.ShapeDtypeStruct((half, PAIR), F32)
    out_shape = jax.ShapeDtypeStruct((length, width), BF16)

    state, iq, ik, iv = call(
        functools.partial(states_kernel, early), (state_shape, wide, wide, wide), 4
    )(queries, keys, values, out_grad)
    both = lax.all_gather(state, "ctx", axis_index_groups=pairs)
    mine = call(chip_sum_kernel, half_shape, 1)(both)

    def exchange(x):
        x = x.reshape(chips, half // chips, PAIR)
        return lax.all_to_all(x, "ctx", 0, 0, axis_index_groups=across).reshape(half, PAIR)

    part = exchange(mine)
    part = call(functools.partial(scan_kernel, chips, lead), half_shape, 1)(part)
    carry = exchange(part)
    carry = lax.all_gather(carry, "ctx", axis_index_groups=pairs)
    return call(
        functools.partial(final_kernel, early),
        (out_shape, out_shape, out_shape),
        9,
        [pltpu.VMEM((length, width), F32)] * 3,
    )(queries, keys, values, out_grad, both, carry, iq, ik, iv)


def solution(mesh):
    spec = P("ctx", "head")
    return jax.shard_map(
        body, mesh=mesh, in_specs=(spec,) * 4, out_specs=(spec,) * 3, check_vma=False
    )
```

time: 393 us -> 51.8 us (0.13); the launches traced: 388 us -> 51.5 us
  other arithmetic: 241 us -> 0 us
  waiting for transfers between devices: 106 us -> 0 us
  blocking collectives: 0 us -> 43.2 us
  local copies, waits for them, and re-layouts: 18.5 us -> 3.8 us
  between operations: 14.2 us -> 0.67 us
  loops' own time: 5.79 us -> 0 us
    select_n x254 -> x0, other arithmetic: 241 us -> none  [turn(): return jnp.where(position < mine, longer, running)]
    all_gather x2 -> x0, waiting for transfers between devices: 106 us -> none  [carried_in(): pieces = lax.all_gather(value, axis)]
    all_to_all x0 -> x2, blocking collectives: none -> 30.6 us  [exchange(): lax.all_to_all(x, 'ctx', 0, 0, axis_index_groups=across).reshape(half, PAIR)]
    all_gather x0 -> x2, blocking collectives: none -> 12.6 us  [the longest x1 8.69 us: body(): both = lax.all_gather(state, 'ctx', axis_index_groups=pairs)]
    rev x1 -> x0, local copies, waits for them, and re-layouts: 11.6 us -> none  [carried_in(): pieces = pieces[::-1]]
    another operation x2 -> x0, loops' own time: 5.79 us -> none  [carried_in(): return lax.fori_loop(0, count - 1, turn, running)]
  transfers between devices with their start and end apart: 2 -> 0, of which waited for: 1 -> 0; matrix products, arithmetic and copies ran while one was open for 35% -> 0% of each run, Pallas kernels for 0% -> 0%
where the time goes in v1:
time: 51.8 us; the launch traced here: 51.5 us
  blocking collectives  43.2 us (83%)
  local copies, waits for them, and re-layouts  3.8 us (7%)
  Pallas kernels  3.8 us (7%)
  between operations  0.67 us (1%)
    all_to_all x2, blocking collectives, exchange(): lax.all_to_all(x, 'ctx', 0, 0, axis_index_groups=across).reshape(half, PAIR)  30.6 us
    all_gather x1, blocking collectives, body(): both = lax.all_gather(state, 'ctx', axis_index_groups=pairs)  8.69 us
    all_gather x1, blocking collectives, body(): carry = lax.all_gather(carry, 'ctx', axis_index_groups=pairs)  3.89 us
    unnamed x12, local copies, waits for them, and re-layouts  3.8 us
    pallas_call x1, Pallas kernels, body(): call(functools.partial(states_kernel, early), (state_shape, wide, wide, w...  2.16 us
    pallas_call x1, Pallas kernels, body(): call(functools.partial(final_kernel, early), (out_shape, out_shape, out_s...  1.29 us

profile of v1, /device:TPU:1, one launch (start us, length us, event | category | flops | bytes accessed | tf_op | source)
XLA Modules:
  0.0 51.5 jit_solution(1288319845003756851)
XLA Ops:
  0.6 0.0 copy-start
  0.6 0.9 %copy-done = bf16[256,512]{1,0:T(8,128)(2,1)S(1)} copy-done((bf16[256,512]{1,0:T(8,128)(2,1)S(1)}, bf16[256,512]{1,0:T(8,128)(2,1)}, u32[]{:S(2)}) %copy-start) | copy-done | bytes 262168
  1.6 0.0 copy-start.2
  1.6 0.9 %copy-done.2 = bf16[256,512]{1,0:T(8,128)(2,1)S(1)} copy-done((bf16[256,512]{1,0:T(8,128)(2,1)S(1)}, bf16[256,512]{1,0:T(8,128)(2,1)}, u32[]{:S(2)}) %copy-start.2) | copy-done | bytes 262168
  2.5 0.0 copy-start.3
  2.5 0.9 %copy-done.3 = bf16[256,512]{1,0:T(8,128)(2,1)S(1)} copy-done((bf16[256,512]{1,0:T(8,128)(2,1)S(1)}, bf16[256,512]{1,0:T(8,128)(2,1)}, u32[]{:S(2)}) %copy-start.3) | copy-done | bytes 262168
  3.5 0.0 copy-start.5
  3.5 0.9 %copy-done.5 = bf16[256,512]{1,0:T(8,128)(2,1)S(1)} copy-done((bf16[256,512]{1,0:T(8,128)(2,1)S(1)}, bf16[256,512]{1,0:T(8,128)(2,1)}, u32[]{:S(2)}) %copy-start.5) | copy-done | bytes 262168
  4.4 2.2 %shard_map.67 = (f32[512,128]{1,0:T(8,128)S(1)}, f32[256,512]{1,0:T(8,128)S(1)}, f32[256,512]{1,0:T(8,128)S(1)}, f32[256,512]{1,0:T(8,128)S(1)}) custom-call(bf16[256,512]{1,0:T(8,128)(2,1)S(1)} %copy-done, bf16[256,512]{1,0:T(8,128)(2,1)S(1)} %copy-done.2, bf16[256,512]{1,0:T(8,128)(2,1)S(1)} %copy-done.3, bf16[256,512]{1,0:T(8,128)(2,1)S(1)} %copy-done.5), custom_call_target="tpu_custom_call" | custom-call | tf_op jit(solution)/shard_map/pallas_call | solution.py:177
  6.6 8.7 %all-gather = f32[1024,128]{1,0:T(8,128)S(1)} all-gather(f32[512,128]{1,0:T(8,128)S(1)} %get-tuple-element.7), channel_id=2, replica_groups={{0,4},{8,12},{16,20},{24,28},{32,36},{40,44},{48,52},{56,60},{64,68},{7..., dimensions={0}, use_global_device_ids=true | all-gather | bytes 786432 | tf_op jit(solution)/shard_map/all_gather | solution.py:180
  15.3 15.4 %all_to_all.10 = f32[64,4,128]{2,1,0:T(4,128)S(1)} all-to-all(f32[64,4,128]{2,1,0:T(4,128)S(1)} %bitcast.7), channel_id=1, replica_groups={{288,296,304,312,320,328,336,344,352,360,368,376,384,392,400,408,416,42..., dimensions={0} | all-to-all | bytes 262144 | tf_op jit(solution)/shard_map/all_to_all | solution.py:185
  30.7 0.3 shard_map.69
  31.1 0.0 copy-start.4
  31.1 15.2 %all_to_all.11 = f32[64,4,128]{2,1,0:T(4,128)S(1)} all-to-all(f32[64,4,128]{2,1,0:T(4,128)S(1)} %bitcast.9), channel_id=1, replica_groups={{288,296,304,312,320,328,336,344,352,360,368,376,384,392,400,408,416,42..., dimensions={0} | all-to-all | bytes 262144 | tf_op jit(solution)/shard_map/all_to_all | solution.py:185
  46.3 0.0 copy-start.1
  46.3 3.9 %all_gather.11.carry_ref = f32[2,256,128]{2,1,0:T(8,128)S(1)} all-gather(f32[1,256,128]{2,1,0:T(8,128)S(1)} %bitcast.10), channel_id=1, replica_groups={{0,4},{8,12},{16,20},{24,28},{32,36},{40,44},{48,52},{56,60},{64,68},{7..., dimensions={0}, use_global_device_ids=true | all-gather | bytes 393216 | tf_op jit(solution)/shard_map/all_gather | solution.py:190
  50.2 0.0 copy-done.4
  50.2 0.0 copy-done.1
  50.2 1.3 %shard_map.70 = (bf16[256,512]{1,0:T(8,128)(2,1)}, bf16[256,512]{1,0:T(8,128)(2,1)}, bf16[256,512]{1,0:T(8,128)(2,1)}) custom-call(bf16[256,512]{1,0:T(8,128)(2,1)S(1)} %copy-done.1, bf16[256,512]{1,0:T(8,128)(2,1)S(1)} %copy-done.2, bf16[256,512]{1,0:T(8,128)(2,1)S(1)} %copy-done.4, bf16[256,512]{1,0:T(8,128)(2,1)S(1)} %copy-done.5, ...), custom_call_target="tpu_custom_call" | custom-call | tf_op jit(solution)/shard_map/pallas_call | solution.py:191
  (1 shorter events, 0.0 us)
Async XLA Ops:
  0.6 1.0 %copy-start = (bf16[256,512]{1,0:T(8,128)(2,1)S(1)}, bf16[256,512]{1,0:T(8,128)(2,1)}, u32[]{:S(2)}) copy-start(bf16[256,512]{1,0:T(8,128)(2,1)} %q_ref.3) | copy-start | bytes 786436
  1.6 0.9 %copy-start.2 = (bf16[256,512]{1,0:T(8,128)(2,1)S(1)}, bf16[256,512]{1,0:T(8,128)(2,1)}, u32[]{:S(2)}) copy-start(bf16[256,512]{1,0:T(8,128)(2,1)} %k_ref.3) | copy-start | bytes 786436
  2.5 0.9 %copy-start.3 = (bf16[256,512]{1,0:T(8,128)(2,1)S(1)}, bf16[256,512]{1,0:T(8,128)(2,1)}, u32[]{:S(2)}) copy-start(bf16[256,512]{1,0:T(8,128)(2,1)} %v_ref.3) | copy-start | bytes 786436
  3.5 0.9 %copy-start.5 = (bf16[256,512]{1,0:T(8,128)(2,1)S(1)}, bf16[256,512]{1,0:T(8,128)(2,1)}, u32[]{:S(2)}) copy-start(bf16[256,512]{1,0:T(8,128)(2,1)} %d_ref.3) | copy-start | bytes 786436
  31.1 19.1 %copy-start.4 = (bf16[256,512]{1,0:T(8,128)(2,1)S(1)}, bf16[256,512]{1,0:T(8,128)(2,1)}, u32[]{:S(2)}) copy-start(bf16[256,512]{1,0:T(8,128)(2,1)} %v_ref.3) | copy-start | bytes 786436
  46.3 3.9 %copy-start.1 = (bf16[256,512]{1,0:T(8,128)(2,1)S(1)}, bf16[256,512]{1,0:T(8,128)(2,1)}, u32[]{:S(2)}) copy-start(bf16[256,512]{1,0:T(8,128)(2,1)} %q_ref.3) | copy-start | bytes 786436

commit v2 on v1

--- a/solution.py
+++ b/solution.py
@@ -66,21 +66,35 @@
             out_ref[pl.ds(base + (2 * g + j) * DH, DH), :] = jnp.where(low, top, bottom)
 
 
-def states_kernel(early, q_ref, k_ref, v_ref, d_ref, state_ref, dq_ref, dk_ref, dv_ref):
+def states_kernel(q_hbm, k_hbm, v_hbm, d_hbm, state_ref, q_ref, k_ref, v_ref, d_ref, sems):
     half = state_ref.shape[0] // 2
+    copies = [
+        pltpu.make_async_copy(src, dst, sems.at[i])
+        for i, (src, dst) in enumerate(
+            ((k_hbm, k_ref), (v_hbm, v_ref), (q_hbm, q_ref), (d_hbm, d_ref))
+        )
+    ]
+    for copy in copies:
+        copy.start()
+    for copy in copies[:2]:
+        copy.wait()
     packed_state(k_ref, v_ref, state_ref, 0)
+    for copy in copies[2:]:
+        copy.wait()
     packed_state(q_ref, d_ref, state_ref, half)
 
-    @pl.when(lax.axis_index("ctx") < early)
-    def _():
-        in_block(q_ref, k_ref, v_ref, d_ref, dq_ref, dk_ref, dv_ref)
-
-
-def chip_sum_kernel(both_ref, sum_ref):
+
+def chip_sum_kernel(
+    early, both_ref, q_ref, k_ref, v_ref, d_ref, sum_ref, dq_ref, dk_ref, dv_ref
+):
     half = sum_ref.shape[0]
     core = lax.axis_index("ctx") % 2
     at = pl.ds(pl.multiple_of(core * half, half), half)
     sum_ref[...] = both_ref[0, at, :] + both_ref[1, at, :]
+
+    @pl.when(lax.axis_index("ctx") < early)
+    def _():
+        in_block(q_ref, k_ref, v_ref, d_ref, dq_ref, dk_ref, dv_ref)
 
 
 def scan_kernel(chips, lead, part_ref, out_ref):
@@ -147,14 +161,14 @@
         finish(dq_ref, dk_ref, dv_ref)
 
 
-def call(kernel, outs, n_in, scratch=(), out_space=VMEM):
+def call(kernel, outs, n_in, scratch=(), in_space=VMEM, grant=24):
     return pl.pallas_call(
         kernel,
         out_shape=outs,
-        in_specs=[pl.BlockSpec(memory_space=VMEM)] * n_in,
-        out_specs=jax.tree.map(lambda _: pl.BlockSpec(memory_space=out_space), outs),
+        in_specs=[pl.BlockSpec(memory_space=in_space)] * n_in,
+        out_specs=jax.tree.map(lambda _: pl.BlockSpec(memory_space=VMEM), outs),
         scratch_shapes=scratch,
-        compiler_params=pltpu.CompilerParams(vmem_limit_bytes=24 * 1024 * 1024),
+        compiler_params=pltpu.CompilerParams(vmem_limit_bytes=int(grant * 2**20)),
     )
 
 
@@ -174,11 +188,19 @@
     half_shape = jax.ShapeDtypeStruct((half, PAIR), F32)
     out_shape = jax.ShapeDtypeStruct((length, width), BF16)
 
-    state, iq, ik, iv = call(
-        functools.partial(states_kernel, early), (state_shape, wide, wide, wide), 4
-    )(queries, keys, values, out_grad)
+    local = (queries, keys, values, out_grad)
+    state = call(
+        states_kernel,
+        state_shape,
+        4,
+        [pltpu.VMEM((length, width), BF16)] * 4 + [pltpu.SemaphoreType.DMA((4,))],
+        in_space=pltpu.HBM,
+        grant=53.5,
+    )(*local)
     both = lax.all_gather(state, "ctx", axis_index_groups=pairs)
-    mine = call(chip_sum_kernel, half_shape, 1)(both)
+    mine, *partial = call(
+        functools.partial(chip_sum_kernel, early), (half_shape,) + (wide,) * 3, 5
+    )(both, *local)
 
     def exchange(x):
         x = x.reshape(chips, half // chips, PAIR)
@@ -193,7 +215,7 @@
         (out_shape, out_shape, out_shape),
         9,
         [pltpu.VMEM((length, width), F32)] * 3,
-    )(queries, keys, values, out_grad, both, carry, iq, ik, iv)
+    )(*local, both, carry, *partial)
 
 
 def solution(mesh):

time: 51.8 us -> 49.1 us (0.948)
  local copies, waits for them, and re-layouts: 3.8 us -> 0.02 us
  Pallas kernels: 3.8 us -> 5.12 us
    unnamed x12 -> x8, local copies, waits for them, and re-layouts: 3.8 us -> 0.02 us
    pallas_call x2, Pallas kernels: 2.17 us -> 3.49 us  [the longest x1 1.84 us: body(): call(functools.partial(chip_sum_kernel, early), (half_shape,) + (wide,) *...]
where the time goes in v2:
time: 49.1 us; the launch traced here: 48.9 us
  blocking collectives  43.1 us (88%)
  Pallas kernels  5.12 us (10%)
  between operations  0.69 us (1%)
    all_to_all x2, blocking collectives, exchange(): lax.all_to_all(x, 'ctx', 0, 0, axis_index_groups=across).reshape(half, PAIR)  30.5 us
    all_gather x1, blocking collectives, body(): both = lax.all_gather(state, 'ctx', axis_index_groups=pairs)  8.82 us
    all_gather x1, blocking collectives, body(): carry = lax.all_gather(carry, 'ctx', axis_index_groups=pairs)  3.76 us
    pallas_call x1, Pallas kernels, body(): call(functools.partial(chip_sum_kernel, early), (half_shape,) + (wide,) *...  1.84 us
    pallas_call x1, Pallas kernels, body(): call(states_kernel, state_shape, 4, [pltpu.VMEM((length, width), BF16)] *...  1.65 us
    pallas_call x1, Pallas kernels, body(): call(functools.partial(final_kernel, early), (out_shape, out_shape, out_s...  1.29 us

profile of v2, /device:TPU:1, one launch (start us, length us, event | category | flops | bytes accessed | tf_op | source)
XLA Modules:
  0.0 48.9 jit_solution(18300686483575776326)
XLA Ops:
  0.6 0.0 copy-start.3
  0.6 1.7 %shard_map.67 = f32[512,128]{1,0:T(8,128)S(1)} custom-call(bf16[256,512]{1,0:T(8,128)(2,1)} %q_ref.3, bf16[256,512]{1,0:T(8,128)(2,1)} %k_ref.3, bf16[256,512]{1,0:T(8,128)(2,1)} %v_ref.3, bf16[256,512]{1,0:T(8,128)(2,1)} %d_ref.3), custom_call_target="tpu_custom_call" | custom-call | tf_op jit(solution)/shard_map/pallas_call | solution.py:192
  2.3 0.0 copy-start
  2.3 0.0 copy-start.1
  2.3 0.0 copy-start.2
  2.3 8.8 %all-gather = f32[1024,128]{1,0:T(8,128)S(1)} all-gather(f32[512,128]{1,0:T(8,128)S(1)} %shard_map.67), channel_id=2, replica_groups={{0,4},{8,12},{16,20},{24,28},{32,36},{40,44},{48,52},{56,60},{64,68},{7..., dimensions={0}, use_global_device_ids=true | all-gather | bytes 786432 | tf_op jit(solution)/shard_map/all_gather | solution.py:200
  11.2 0.0 copy-done.3
  11.2 0.0 copy-done
  11.2 0.0 copy-done.1
  11.2 0.0 copy-done.2
  11.2 1.8 %shard_map.68 = (f32[256,128]{1,0:T(8,128)S(1)}, f32[256,512]{1,0:T(8,128)S(1)}, f32[256,512]{1,0:T(8,128)S(1)}, f32[256,512]{1,0:T(8,128)S(1)}) custom-call(f32[2,512,128]{2,1,0:T(8,128)S(1)} %bitcast.5, bf16[256,512]{1,0:T(8,128)(2,1)S(1)} %copy-done, bf16[256,512]{1,0:T(8,128)(2,1)S(1)} %copy-done.1, bf16[256,512]{1,0:T(8,128)(2,1)S(1)} %copy-done.2, ...), custom_call_target="tpu_custom_call" | custom-call | tf_op jit(solution)/shard_map/pallas_call | solution.py:201
  13.0 15.4 %all_to_all.10 = f32[64,4,128]{2,1,0:T(4,128)S(1)} all-to-all(f32[64,4,128]{2,1,0:T(4,128)S(1)} %bitcast.9), channel_id=1, replica_groups={{288,296,304,312,320,328,336,344,352,360,368,376,384,392,400,408,416,42..., dimensions={0} | all-to-all | bytes 262144 | tf_op jit(solution)/shard_map/all_to_all | solution.py:207
  28.4 0.3 shard_map.69
  28.8 15.1 %all_to_all.11 = f32[64,4,128]{2,1,0:T(4,128)S(1)} all-to-all(f32[64,4,128]{2,1,0:T(4,128)S(1)} %bitcast.8), channel_id=1, replica_groups={{288,296,304,312,320,328,336,344,352,360,368,376,384,392,400,408,416,42..., dimensions={0} | all-to-all | bytes 262144 | tf_op jit(solution)/shard_map/all_to_all | solution.py:207
  43.8 3.8 %all_gather.11.carry_ref = f32[2,256,128]{2,1,0:T(8,128)S(1)} all-gather(f32[1,256,128]{2,1,0:T(8,128)S(1)} %bitcast.10), channel_id=1, replica_groups={{0,4},{8,12},{16,20},{24,28},{32,36},{40,44},{48,52},{56,60},{64,68},{7..., dimensions={0}, use_global_device_ids=true | all-gather | bytes 393216 | tf_op jit(solution)/shard_map/all_gather | solution.py:212
  47.6 1.3 %shard_map.70 = (bf16[256,512]{1,0:T(8,128)(2,1)}, bf16[256,512]{1,0:T(8,128)(2,1)}, bf16[256,512]{1,0:T(8,128)(2,1)}) custom-call(bf16[256,512]{1,0:T(8,128)(2,1)S(1)} %copy-done, bf16[256,512]{1,0:T(8,128)(2,1)S(1)} %copy-done.1, bf16[256,512]{1,0:T(8,128)(2,1)S(1)} %copy-done.2, bf16[256,512]{1,0:T(8,128)(2,1)S(1)} %copy-done.3, ...), custom_call_target="tpu_custom_call" | custom-call | tf_op jit(solution)/shard_map/pallas_call | solution.py:213
Async XLA Ops:
  0.6 10.5 %copy-start.3 = (bf16[256,512]{1,0:T(8,128)(2,1)S(1)}, bf16[256,512]{1,0:T(8,128)(2,1)}, u32[]{:S(2)}) copy-start(bf16[256,512]{1,0:T(8,128)(2,1)} %d_ref.3) | copy-start | bytes 786436
  2.3 8.9 %copy-start = (bf16[256,512]{1,0:T(8,128)(2,1)S(1)}, bf16[256,512]{1,0:T(8,128)(2,1)}, u32[]{:S(2)}) copy-start(bf16[256,512]{1,0:T(8,128)(2,1)} %q_ref.3) | copy-start | bytes 786436
  2.3 8.9 %copy-start.1 = (bf16[256,512]{1,0:T(8,128)(2,1)S(1)}, bf16[256,512]{1,0:T(8,128)(2,1)}, u32[]{:S(2)}) copy-start(bf16[256,512]{1,0:T(8,128)(2,1)} %k_ref.3) | copy-start | bytes 786436
  2.3 8.8 %copy-start.2 = (bf16[256,512]{1,0:T(8,128)(2,1)S(1)}, bf16[256,512]{1,0:T(8,128)(2,1)}, u32[]{:S(2)}) copy-start(bf16[256,512]{1,0:T(8,128)(2,1)} %v_ref.3) | copy-start | bytes 786436

commit v3 on v2

v3 whole, which is shorter than its diff:
```python
import functools

import jax
import jax.numpy as jnp
from jax import lax
from jax.experimental import pallas as pl
from jax.experimental.pallas import tpu as pltpu
from jax.sharding import PartitionSpec as P

DH = 64
PAIR = 2 * DH
QUAD = 4 * DH
GRANT = 53.5
VMEM = pltpu.VMEM
F32 = jnp.float32
BF16 = jnp.bfloat16
NT = (((1,), (1,)), ((), ()))
NN = (((1,), (0,)), ((), ()))
TN = (((0,), (0,)), ((), ()))


def dot(a, b, dims):
    return lax.dot_general(a, b, dims, preferred_element_type=F32)


def low_lanes(shape):
    return (lax.broadcasted_iota(jnp.int32, shape, 1) & DH) == 0


def in_block(q_ref, k_ref, v_ref, d_ref, dq_ref, dk_ref, dv_ref):
    length, width = q_ref.shape
    rows = lax.broadcasted_iota(jnp.int32, (length, length), 0)
    cols = lax.broadcasted_iota(jnp.int32, (length, length), 1)
    keep = rows >= cols
    keep_t = cols >= rows
    low = low_lanes((length, PAIR))

    def pair(p, _):
        at = pl.ds(p * PAIR, PAIR)
        q, k, v, d = q_ref[:, at], k_ref[:, at], v_ref[:, at], d_ref[:, at]
        dq = dk = dv = 0.0
        for mine in (low, ~low):
            kh = jnp.where(mine, k, 0)
            vh = jnp.where(mine, v, 0)
            qh = jnp.where(mine, q, 0)
            dh = jnp.where(mine, d, 0)
            b = jnp.where(keep, dot(d, vh, NT), 0.0).astype(BF16)
            bt = jnp.where(keep_t, dot(v, dh, NT), 0.0).astype(BF16)
            at_ = jnp.where(keep_t, dot(k, qh, NT), 0.0).astype(BF16)
            dq += dot(b, kh, NN)
            dk += dot(bt, qh, NN)
            dv += dot(at_, dh, NN)
        dq_ref[:, at] = dq
        dk_ref[:, at] = dk
        dv_ref[:, at] = dv
        return 0

    [pair(p, 0) for p in range(width // PAIR)]


def packed_state(a_ref, b_ref, mine, own_ref, send_ref):
    width = a_ref.shape[1]
    low = low_lanes((DH, PAIR))
    blocks = []
    for g in range(width // QUAD):
        at = pl.ds(g * QUAD, QUAD)
        full = dot(a_ref[:, at], b_ref[:, at], TN)
        for j in range(2):
            lanes = slice(j * PAIR, (j + 1) * PAIR)
            top = full[j * PAIR : j * PAIR + DH, lanes]
            bottom = full[j * PAIR + DH : (j + 1) * PAIR, lanes]
            blocks.append(jnp.where(low, top, bottom))

    def store(ref):
        for p, block in enumerate(blocks):
            ref[pl.ds(p * DH, DH), :] = block

    pl.when(mine)(functools.partial(store, own_ref))
    pl.when(jnp.logical_not(mine))(functools.partial(store, send_ref))


def states_kernel(
    q_hbm, k_hbm, v_hbm, d_hbm, own_ref, send_ref, q_ref, k_ref, v_ref, d_ref, sems
):
    core = lax.axis_index("ctx") % 2
    copies = [
        pltpu.make_async_copy(src, dst, sems.at[i])
        for i, (src, dst) in enumerate(
            ((k_hbm, k_ref), (v_hbm, v_ref), (q_hbm, q_ref), (d_hbm, d_ref))
        )
    ]
    for copy in copies:
        copy.start()
    for copy in copies[:2]:
        copy.wait()
    packed_state(k_ref, v_ref, core == 0, own_ref, send_ref)
    for copy in copies[2:]:
        copy.wait()
    packed_state(q_ref, d_ref, core == 1, own_ref, send_ref)


def chip_sum_kernel(
    early, own_ref, sent_ref, q_ref, k_ref, v_ref, d_ref, sum_ref, dq_ref, dk_ref, dv_ref
):
    core = lax.axis_index("ctx") % 2
    sum_ref[...] = own_ref[...] + sent_ref[1 - core]

    @pl.when(lax.axis_index("ctx") < early)
    def _():
        in_block(q_ref, k_ref, v_ref, d_ref, dq_ref, dk_ref, dv_ref)


def add_own_kernel(carry_ref, own_ref, out_ref):
    out_ref[...] = carry_ref[...] + own_ref[...]


def scan_kernel(order, part_ref, out_ref):
    chips = len(order)
    each = part_ref.shape[0] // chips
    slot = {chip: s for s, chip in enumerate(order)}

    def scan(sequence):
        total = jnp.zeros((each, PAIR), F32)
        for chip in sequence:
            at = pl.ds(slot[chip] * each, each)
            out_ref[at, :] = total
            total = total + part_ref[at, :]

    core = lax.axis_index("ctx") % 2

    @pl.when(core == 0)
    def _():
        scan(range(chips))

    @pl.when(core == 1)
    def _():
        scan(reversed(range(chips)))


def block_diagonal(packed, g):
    low = low_lanes((DH, PAIR))
    zero = jnp.zeros((PAIR, PAIR), BF16)
    blocks = []
    for j in range(2):
        two = packed[(2 * g + j) * DH : (2 * g + j + 1) * DH]
        blocks.append(
            jnp.concatenate([jnp.where(low, two, 0.0), jnp.where(low, 0.0, two)], axis=0).astype(BF16)
        )
    return jnp.concatenate(
        [
            jnp.concatenate([blocks[0], zero], axis=1),
            jnp.concatenate([zero, blocks[1]], axis=1),
        ],
        axis=0,
    )


def final_kernel(
    early, q_ref, k_ref, v_ref, d_ref, carry_ref, other_ref, iq_ref, ik_ref, iv_ref,
    oq_hbm, ok_hbm, ov_hbm, dq_ref, dk_ref, dv_ref, oq_ref, ok_ref, ov_ref, sems,
):
    width = q_ref.shape[1]
    me = lax.axis_index("ctx")
    core = me % 2

    def finish(sq_ref, sk_ref, sv_ref):
        prefix = jnp.where(core == 0, carry_ref[...], other_ref[0])
        suffix = jnp.where(core == 1, carry_ref[...], other_ref[1])
        copies = []
        for g in range(width // QUAD):
            at = pl.ds(g * QUAD, QUAD)
            pre, suf = block_diagonal(prefix, g), block_diagonal(suffix, g)
            for i, (own, sum_ref, x_ref, state, dims, hbm) in enumerate((
                (oq_ref, sq_ref, d_ref, pre, NT, oq_hbm),
                (ok_ref, sk_ref, v_ref, suf, NT, ok_hbm),
                (ov_ref, sv_ref, k_ref, suf, NN, ov_hbm),
            )):
                own[:, at] = (sum_ref[:, at] + dot(x_ref[:, at], state, dims)).astype(BF16)
                copy = pltpu.make_async_copy(own.at[:, at], hbm.at[:, at], sems.at[i, g])
                copy.start()
                copies.append(copy)
        for copy in copies:
            copy.wait()

    @pl.when(me < early)
    def _():
        finish(iq_ref, ik_ref, iv_ref)

    @pl.when(me >= early)
    def _():
        in_block(q_ref, k_ref, v_ref, d_ref, dq_ref, dk_ref, dv_ref)
        finish(dq_ref, dk_ref, dv_ref)


def call(kernel, outs, n_in, scratch=(), in_space=VMEM, out_space=VMEM, grant=24):
    return pl.pallas_call(
        kernel,
        out_shape=outs,
        in_specs=[pl.BlockSpec(memory_space=in_space)] * n_in,
        out_specs=jax.tree.map(lambda _: pl.BlockSpec(memory_space=out_space), outs),
        scratch_shapes=scratch,
        compiler_params=pltpu.CompilerParams(vmem_limit_bytes=int(grant * 2**20)),
    )


def body(queries, keys, values, out_grad):
    length, width = queries.shape
    half = width // 2
    count = lax.axis_size("ctx")
    chips = count // 2
    early = count // 2
    lead = chips // 2 + 4
    order = [(s + lead) % chips for s in range(chips)]
    pairs = [[2 * c, 2 * c + 1] for c in range(chips)]
    across = [[2 * c + core for c in order] for core in range(2)]

    wide = jax.ShapeDtypeStruct((length, width), F32)
    half_shape = jax.ShapeDtypeStruct((half, PAIR), F32)
    out_shape = jax.ShapeDtypeStruct((length, width), BF16)

    local = (queries, keys, values, out_grad)
    own, send = call(
        states_kernel,
        (half_shape, half_shape),
        4,
        [pltpu.VMEM((length, width), BF16)] * 4 + [pltpu.SemaphoreType.DMA((4,))],
        in_space=pltpu.HBM,
        grant=GRANT,
    )(*local)
    sent = lax.all_gather(send, "ctx", axis_index_groups=pairs)
    mine, *partial = call(
        functools.partial(chip_sum_kernel, early), (half_shape,) + (wide,) * 3, 6
    )(own, sent, *local)

    def exchange(x):
        x = x.reshape(chips, half // chips, PAIR)
        return lax.all_to_all(x, "ctx", 0, 0, axis_index_groups=across).reshape(half, PAIR)

    part = exchange(mine)
    part = call(functools.partial(scan_kernel, order), half_shape, 1)(part)
    carry = exchange(part)
    other = call(add_own_kernel, half_shape, 2)(carry, own)
    other = lax.all_gather(other, "ctx", axis_index_groups=pairs)
    return call(
        functools.partial(final_kernel, early),
        (out_shape, out_shape, out_shape),
        9,
        [pltpu.VMEM((length, width), F32)] * 3
        + [pltpu.VMEM((length, width), BF16)] * 3
        + [pltpu.SemaphoreType.DMA((3, width // QUAD))],
        out_space=pltpu.HBM,
    )(*local, carry, other, *partial)


def solution(mesh):
    spec = P("ctx", "head")
    return jax.shard_map(
        body, mesh=mesh, in_specs=(spec,) * 4, out_specs=(spec,) * 3, check_vma=False
    )
```

time: 49.1 us -> 48.6 us (0.990)
    pallas_call x2 -> x3, Pallas kernels: 1.99 us -> 1.77 us  [the longest x1 1.68 us: body(): call(states_kernel, (half_shape, half_shape), 4, [pltpu.VMEM((length, wid...]
where the time goes in v3:
time: 48.6 us; the launch traced here: 48.4 us
  blocking collectives  42.9 us (88%)
  Pallas kernels  4.8 us (10%)
  between operations  0.69 us (1%)
    all_to_all x2, blocking collectives, exchange(): lax.all_to_all(x, 'ctx', 0, 0, axis_index_groups=across).reshape(half, PAIR)  30.5 us
    all_gather x1, blocking collectives, body(): sent = lax.all_gather(send, 'ctx', axis_index_groups=pairs)  8.64 us
    all_gather x1, blocking collectives, body(): other = lax.all_gather(other, 'ctx', axis_index_groups=pairs)  3.77 us
    pallas_call x1, Pallas kernels, body(): call(functools.partial(chip_sum_kernel, early), (half_shape,) + (wide,) *...  1.83 us
    pallas_call x1, Pallas kernels, body(): call(states_kernel, (half_shape, half_shape), 4, [pltpu.VMEM((length, wid...  1.68 us
    pallas_call x1, Pallas kernels, body(): call(functools.partial(final_kernel, early), (out_shape, out_shape, out_s...  1.2 us

profile of v3, /device:TPU:1, one launch (start us, length us, event | category | flops | bytes accessed | tf_op | source)
XLA Modules:
  0.0 48.4 jit_solution(9847553724754613925)
XLA Ops:
  0.6 0.0 copy-start.1
  0.6 0.0 copy-start.2
  0.7 0.0 copy-start.3
  0.7 1.7 %shard_map.67 = (f32[256,128]{1,0:T(8,128)S(1)}, f32[256,128]{1,0:T(8,128)S(1)}) custom-call(bf16[256,512]{1,0:T(8,128)(2,1)} %q_ref.3, bf16[256,512]{1,0:T(8,128)(2,1)} %k_ref.3, bf16[256,512]{1,0:T(8,128)(2,1)} %v_ref.3, bf16[256,512]{1,0:T(8,128)(2,1)} %d_ref.3), custom_call_target="tpu_custom_call" | custom-call | tf_op jit(solution)/shard_map/pallas_call | solution.py:222
  2.4 0.0 copy-start
  2.4 8.6 %all-gather = f32[512,128]{1,0:T(8,128)S(1)} all-gather(f32[256,128]{1,0:T(8,128)S(1)} %get-tuple-element.10), channel_id=2, replica_groups={{0,4},{8,12},{16,20},{24,28},{32,36},{40,44},{48,52},{56,60},{64,68},{7..., dimensions={0}, use_global_device_ids=true | all-gather | bytes 393216 | tf_op jit(solution)/shard_map/all_gather | solution.py:230
  11.0 0.0 copy-done.1
  11.0 0.0 copy-done.2
  11.0 0.0 copy-done.3
  11.0 0.0 copy-done
  11.0 1.8 %shard_map.68 = (f32[256,128]{1,0:T(8,128)S(1)}, f32[256,512]{1,0:T(8,128)S(1)}, f32[256,512]{1,0:T(8,128)S(1)}, f32[256,512]{1,0:T(8,128)S(1)}) custom-call(f32[256,128]{1,0:T(8,128)S(1)} %get-tuple-element.9.own_ref, f32[2,256,128]{2,1,0:T(8,128)S(1)} %bitcast.9, bf16[256,512]{1,0:T(8,128)(2,1)S(1)} %copy-done, bf16[256,512]{1,0:T(8,128)(2,1)S(1)} %copy-done.1, ...), custom_call_target="tpu_custom_call" | custom-call | tf_op jit(solution)/shard_map/pallas_call | solution.py:231
  12.9 15.4 %all_to_all.10 = f32[64,4,128]{2,1,0:T(4,128)S(1)} all-to-all(f32[64,4,128]{2,1,0:T(4,128)S(1)} %bitcast.12), channel_id=1, replica_groups={{288,296,304,312,320,328,336,344,352,360,368,376,384,392,400,408,416,42..., dimensions={0} | all-to-all | bytes 262144 | tf_op jit(solution)/shard_map/all_to_all | solution.py:237
  28.3 0.1 shard_map.69
  28.4 15.1 %all_to_all.11 = f32[64,4,128]{2,1,0:T(4,128)S(1)} all-to-all(f32[64,4,128]{2,1,0:T(4,128)S(1)} %bitcast.11), channel_id=1, replica_groups={{288,296,304,312,320,328,336,344,352,360,368,376,384,392,400,408,416,42..., dimensions={0} | all-to-all | bytes 262144 | tf_op jit(solution)/shard_map/all_to_all | solution.py:237
  43.4 3.8 %all-gather.1 = f32[512,128]{1,0:T(8,128)S(1)} all-gather(f32[256,128]{1,0:T(8,128)S(1)} %shard_map.70), channel_id=3, replica_groups={{0,4},{8,12},{16,20},{24,28},{32,36},{40,44},{48,52},{56,60},{64,68},{7..., dimensions={0}, use_global_device_ids=true | all-gather | bytes 393216 | tf_op jit(solution)/shard_map/all_gather | solution.py:243
  47.2 1.2 %shard_map.71 = (bf16[256,512]{1,0:T(8,128)(2,1)}, bf16[256,512]{1,0:T(8,128)(2,1)}, bf16[256,512]{1,0:T(8,128)(2,1)}) custom-call(bf16[256,512]{1,0:T(8,128)(2,1)S(1)} %copy-done, bf16[256,512]{1,0:T(8,128)(2,1)S(1)} %copy-done.1, bf16[256,512]{1,0:T(8,128)(2,1)S(1)} %copy-done.2, bf16[256,512]{1,0:T(8,128)(2,1)S(1)} %copy-done.3, f32[256,128]{1,0:T(8,128)S(1)} %bitcast.7, ...), custom_call_target="tpu_custom_call" | custom-call | tf_op jit(solution)/shard_map/pallas_call | solution.py:244
  (1 shorter events, 0.0 us)
Async XLA Ops:
  0.6 10.4 %copy-start.1 = (bf16[256,512]{1,0:T(8,128)(2,1)S(1)}, bf16[256,512]{1,0:T(8,128)(2,1)}, u32[]{:S(2)}) copy-start(bf16[256,512]{1,0:T(8,128)(2,1)} %k_ref.3) | copy-start | bytes 786436
  0.6 10.4 %copy-start.2 = (bf16[256,512]{1,0:T(8,128)(2,1)S(1)}, bf16[256,512]{1,0:T(8,128)(2,1)}, u32[]{:S(2)}) copy-start(bf16[256,512]{1,0:T(8,128)(2,1)} %v_ref.3) | copy-start | bytes 786436
  0.7 10.4 %copy-start.3 = (bf16[256,512]{1,0:T(8,128)(2,1)S(1)}, bf16[256,512]{1,0:T(8,128)(2,1)}, u32[]{:S(2)}) copy-start(bf16[256,512]{1,0:T(8,128)(2,1)} %d_ref.3) | copy-start | bytes 786436
  2.4 8.7 %copy-start = (bf16[256,512]{1,0:T(8,128)(2,1)S(1)}, bf16[256,512]{1,0:T(8,128)(2,1)}, u32[]{:S(2)}) copy-start(bf16[256,512]{1,0:T(8,128)(2,1)} %q_ref.3) | copy-start | bytes 786436

commit v4 on v3

--- a/solution.py
+++ b/solution.py
@@ -110,10 +110,6 @@
         in_block(q_ref, k_ref, v_ref, d_ref, dq_ref, dk_ref, dv_ref)
 
 
-def add_own_kernel(carry_ref, own_ref, out_ref):
-    out_ref[...] = carry_ref[...] + own_ref[...]
-
-
 def scan_kernel(order, part_ref, out_ref):
     chips = len(order)
     each = part_ref.shape[0] // chips
@@ -155,8 +151,25 @@
     )
 
 
+def add_own_kernel(
+    early, carry_ref, own_ref, k_ref, v_ref, ik_ref, iv_ref, out_ref, rk_ref, rv_ref
+):
+    out_ref[...] = carry_ref[...] + own_ref[...]
+    me = lax.axis_index("ctx")
+
+    @pl.when((me < early) & (me % 2 == 1))
+    def _():
+        suffix = carry_ref[...]
+        for g in range(k_ref.shape[1] // QUAD):
+            at = pl.ds(g * QUAD, QUAD)
+            suf = block_diagonal(suffix, g)
+            rk_ref[:, at] = (ik_ref[:, at] + dot(v_ref[:, at], suf, NT)).astype(BF16)
+            rv_ref[:, at] = (iv_ref[:, at] + dot(k_ref[:, at], suf, NN)).astype(BF16)
+
+
 def final_kernel(
     early, q_ref, k_ref, v_ref, d_ref, carry_ref, other_ref, iq_ref, ik_ref, iv_ref,
+    rk_ref, rv_ref,
     oq_hbm, ok_hbm, ov_hbm, dq_ref, dk_ref, dv_ref, oq_ref, ok_ref, ov_ref, sems,
 ):
     width = q_ref.shape[1]
@@ -182,7 +195,26 @@
         for copy in copies:
             copy.wait()
 
-    @pl.when(me < early)
+    @pl.when((me < early) & (core == 1))
+    def _():
+        copies = [
+            pltpu.make_async_copy(rk_ref, ok_hbm, sems.at[1, 0]),
+            pltpu.make_async_copy(rv_ref, ov_hbm, sems.at[2, 0]),
+        ]
+        for copy in copies:
+            copy.start()
+        prefix = other_ref[0]
+        for g in range(width // QUAD):
+            at = pl.ds(g * QUAD, QUAD)
+            pre = block_diagonal(prefix, g)
+            oq_ref[:, at] = (iq_ref[:, at] + dot(d_ref[:, at], pre, NT)).astype(BF16)
+            copy = pltpu.make_async_copy(oq_ref.at[:, at], oq_hbm.at[:, at], sems.at[0, g])
+            copy.start()
+            copies.append(copy)
+        for copy in copies:
+            copy.wait()
+
+    @pl.when((me < early) & (core == 0))
     def _():
         finish(iq_ref, ik_ref, iv_ref)
 
@@ -239,17 +271,19 @@
     part = exchange(mine)
     part = call(functools.partial(scan_kernel, order), half_shape, 1)(part)
     carry = exchange(part)
-    other = call(add_own_kernel, half_shape, 2)(carry, own)
+    other, *ready = call(
+        functools.partial(add_own_kernel, early), (half_shape, out_shape, out_shape), 6
+    )(carry, own, keys, values, *partial[1:])
     other = lax.all_gather(other, "ctx", axis_index_groups=pairs)
     return call(
         functools.partial(final_kernel, early),
         (out_shape, out_shape, out_shape),
-        9,
+        11,
         [pltpu.VMEM((length, width), F32)] * 3
         + [pltpu.VMEM((length, width), BF16)] * 3
         + [pltpu.SemaphoreType.DMA((3, width // QUAD))],
         out_space=pltpu.HBM,
-    )(*local, carry, other, *partial)
+    )(*local, carry, other, *partial, *ready)
 
 
 def solution(mesh):

time: 48.6 us -> 48.4 us (level)
  no operation moved by 1% of the time
where the time goes in v4:
time: 48.4 us; the launch traced here: 48.2 us
  blocking collectives  42.6 us (88%)
  Pallas kernels  4.94 us (10%)
  between operations  0.69 us (1%)
    all_to_all x2, blocking collectives, exchange(): lax.all_to_all(x, 'ctx', 0, 0, axis_index_groups=across).reshape(half, PAIR)  30.5 us
    all_gather x1, blocking collectives, body(): sent = lax.all_gather(send, 'ctx', axis_index_groups=pairs)  8.64 us
    all_gather x1, blocking collectives, body(): other = lax.all_gather(other, 'ctx', axis_index_groups=pairs)  3.45 us
    pallas_call x1, Pallas kernels, body(): call(functools.partial(chip_sum_kernel, early), (half_shape,) + (wide,) *...  1.84 us
    pallas_call x1, Pallas kernels, body(): call(states_kernel, (half_shape, half_shape), 4, [pltpu.VMEM((length, wid...  1.68 us
    pallas_call x1, Pallas kernels, body(): call(functools.partial(final_kernel, early), (out_shape, out_shape, out_s...  1.02 us

profile of v4, /device:TPU:1, one launch (start us, length us, event | category | flops | bytes accessed | tf_op | source)
XLA Modules:
  0.0 48.2 jit_solution(1046899185341036957)
XLA Ops:
  0.6 0.0 copy-start.1
  0.6 0.0 copy-start.2
  0.7 0.0 copy-start.3
  0.7 1.7 %shard_map.67 = (f32[256,128]{1,0:T(8,128)S(1)}, f32[256,128]{1,0:T(8,128)S(1)}) custom-call(bf16[256,512]{1,0:T(8,128)(2,1)} %q_ref.3, bf16[256,512]{1,0:T(8,128)(2,1)} %k_ref.5, bf16[256,512]{1,0:T(8,128)(2,1)} %v_ref.5, bf16[256,512]{1,0:T(8,128)(2,1)} %d_ref.3), custom_call_target="tpu_custom_call" | custom-call | tf_op jit(solution)/shard_map/pallas_call | solution.py:254
  2.4 0.0 copy-start
  2.4 8.6 %all-gather = f32[512,128]{1,0:T(8,128)S(1)} all-gather(f32[256,128]{1,0:T(8,128)S(1)} %get-tuple-element.13), channel_id=2, replica_groups={{0,4},{8,12},{16,20},{24,28},{32,36},{40,44},{48,52},{56,60},{64,68},{7..., dimensions={0}, use_global_device_ids=true | all-gather | bytes 393216 | tf_op jit(solution)/shard_map/all_gather | solution.py:262
  11.0 0.0 copy-done.1
  11.0 0.0 copy-done.2
  11.0 0.0 copy-done.3
  11.0 0.0 copy-done
  11.0 1.8 %shard_map.68 = (f32[256,128]{1,0:T(8,128)S(1)}, f32[256,512]{1,0:T(8,128)S(1)}, f32[256,512]{1,0:T(8,128)S(1)}, f32[256,512]{1,0:T(8,128)S(1)}) custom-call(f32[256,128]{1,0:T(8,128)S(1)} %get-tuple-element.12.own_ref, f32[2,256,128]{2,1,0:T(8,128)S(1)} %bitcast.9, bf16[256,512]{1,0:T(8,128)(2,1)S(1)} %copy-done.2, bf16[256,512]{1,0:T(8,128)(2,1)S(1)} %copy-done, ...), custom_call_target="tpu_custom_call" | custom-call | tf_op jit(solution)/shard_map/pallas_call | solution.py:263
  12.9 15.5 %all_to_all.10 = f32[64,4,128]{2,1,0:T(4,128)S(1)} all-to-all(f32[64,4,128]{2,1,0:T(4,128)S(1)} %bitcast.12), channel_id=1, replica_groups={{288,296,304,312,320,328,336,344,352,360,368,376,384,392,400,408,416,42..., dimensions={0} | all-to-all | bytes 262144 | tf_op jit(solution)/shard_map/all_to_all | solution.py:269
  28.3 0.1 shard_map.69
  28.4 15.0 %all_to_all.11 = f32[64,4,128]{2,1,0:T(4,128)S(1)} all-to-all(f32[64,4,128]{2,1,0:T(4,128)S(1)} %bitcast.11), channel_id=1, replica_groups={{288,296,304,312,320,328,336,344,352,360,368,376,384,392,400,408,416,42..., dimensions={0} | all-to-all | bytes 262144 | tf_op jit(solution)/shard_map/all_to_all | solution.py:269
  43.4 0.3 shard_map.70
  43.8 3.5 %all-gather.1 = f32[512,128]{1,0:T(8,128)S(1)} all-gather(f32[256,128]{1,0:T(8,128)S(1)} %get-tuple-element.17), channel_id=3, replica_groups={{0,4},{8,12},{16,20},{24,28},{32,36},{40,44},{48,52},{56,60},{64,68},{7..., dimensions={0}, use_global_device_ids=true | all-gather | bytes 393216 | tf_op jit(solution)/shard_map/all_gather | solution.py:277
  47.2 1.0 %shard_map.71 = (bf16[256,512]{1,0:T(8,128)(2,1)}, bf16[256,512]{1,0:T(8,128)(2,1)}, bf16[256,512]{1,0:T(8,128)(2,1)}) custom-call(bf16[256,512]{1,0:T(8,128)(2,1)S(1)} %copy-done.2, bf16[256,512]{1,0:T(8,128)(2,1)S(1)} %copy-done, bf16[256,512]{1,0:T(8,128)(2,1)S(1)} %copy-done.1, bf16[256,512]{1,0:T(8,128)(2,1)S(1)} %copy-done.3, f32[256,128]{1,0:T(8,128)S(1)} %bitcast.7, ...), custom_call_target="tpu_custom_call" | custom-call | tf_op jit(solution)/shard_map/pallas_call | solution.py:278
Async XLA Ops:
  0.6 10.4 %copy-start.1 = (bf16[256,512]{1,0:T(8,128)(2,1)S(1)}, bf16[256,512]{1,0:T(8,128)(2,1)}, u32[]{:S(2)}) copy-start(bf16[256,512]{1,0:T(8,128)(2,1)} %v_ref.5) | copy-start | bytes 786436
  0.6 10.4 %copy-start.2 = (bf16[256,512]{1,0:T(8,128)(2,1)S(1)}, bf16[256,512]{1,0:T(8,128)(2,1)}, u32[]{:S(2)}) copy-start(bf16[256,512]{1,0:T(8,128)(2,1)} %q_ref.3) | copy-start | bytes 786436
  0.7 10.4 %copy-start.3 = (bf16[256,512]{1,0:T(8,128)(2,1)S(1)}, bf16[256,512]{1,0:T(8,128)(2,1)}, u32[]{:S(2)}) copy-start(bf16[256,512]{1,0:T(8,128)(2,1)} %d_ref.3) | copy-start | bytes 786436
  2.4 8.7 %copy-start = (bf16[256,512]{1,0:T(8,128)(2,1)S(1)}, bf16[256,512]{1,0:T(8,128)(2,1)}, u32[]{:S(2)}) copy-start(bf16[256,512]{1,0:T(8,128)(2,1)} %k_ref.5) | copy-start | bytes 786436

commit v5 on v4

--- a/solution.py
+++ b/solution.py
@@ -110,12 +110,12 @@
         in_block(q_ref, k_ref, v_ref, d_ref, dq_ref, dk_ref, dv_ref)
 
 
-def scan_kernel(order, part_ref, out_ref):
-    chips = len(order)
+def scan_kernel(orders, part_ref, out_ref):
+    chips = len(orders[0])
     each = part_ref.shape[0] // chips
-    slot = {chip: s for s, chip in enumerate(order)}
-
-    def scan(sequence):
+    slots = [{chip: s for s, chip in enumerate(order)} for order in orders]
+
+    def scan(slot, sequence):
         total = jnp.zeros((each, PAIR), F32)
         for chip in sequence:
             at = pl.ds(slot[chip] * each, each)
@@ -126,11 +126,11 @@
 
     @pl.when(core == 0)
     def _():
-        scan(range(chips))
+        scan(slots[0], range(chips))
 
     @pl.when(core == 1)
     def _():
-        scan(reversed(range(chips)))
+        scan(slots[1], reversed(range(chips)))
 
 
 def block_diagonal(packed, g):
@@ -241,10 +241,10 @@
     count = lax.axis_size("ctx")
     chips = count // 2
     early = count // 2
-    lead = chips // 2 + 4
-    order = [(s + lead) % chips for s in range(chips)]
+    leads = (chips // 2 + 4, chips * 3 // 4 + 4)
+    orders = [[(s + lead) % chips for s in range(chips)] for lead in leads]
     pairs = [[2 * c, 2 * c + 1] for c in range(chips)]
-    across = [[2 * c + core for c in order] for core in range(2)]
+    across = [[2 * c + core for c in orders[core]] for core in range(2)]
 
     wide = jax.ShapeDtypeStruct((length, width), F32)
     half_shape = jax.ShapeDtypeStruct((half, PAIR), F32)
@@ -269,7 +269,7 @@
         return lax.all_to_all(x, "ctx", 0, 0, axis_index_groups=across).reshape(half, PAIR)
 
     part = exchange(mine)
-    part = call(functools.partial(scan_kernel, order), half_shape, 1)(part)
+    part = call(functools.partial(scan_kernel, orders), half_shape, 1)(part)
     carry = exchange(part)
     other, *ready = call(
         functools.partial(add_own_kernel, early), (half_shape, out_shape, out_shape), 6

time: 48.4 us -> 48.5 us (level)
  no operation moved by 1% of the time
where the time goes in v5:
time: 48.5 us; the launch traced here: 48.3 us
  blocking collectives  42.6 us (88%)
  Pallas kernels  4.93 us (10%)
  between operations  0.69 us (1%)
    all_to_all x2, blocking collectives, exchange(): lax.all_to_all(x, 'ctx', 0, 0, axis_index_groups=across).reshape(half, PAIR)  30.7 us
    all_gather x1, blocking collectives, body(): sent = lax.all_gather(send, 'ctx', axis_index_groups=pairs)  8.64 us
    all_gather x1, blocking collectives, body(): other = lax.all_gather(other, 'ctx', axis_index_groups=pairs)  3.3 us
    pallas_call x1, Pallas kernels, body(): call(functools.partial(chip_sum_kernel, early), (half_shape,) + (wide,) *...  1.84 us
    pallas_call x1, Pallas kernels, body(): call(states_kernel, (half_shape, half_shape), 4, [pltpu.VMEM((length, wid...  1.68 us
    pallas_call x1, Pallas kernels, body(): call(functools.partial(final_kernel, early), (out_shape, out_shape, out_s...  1.01 us

profile of v5, /device:TPU:1, one launch (start us, length us, event | category | flops | bytes accessed | tf_op | source)
XLA Modules:
  0.0 48.3 jit_solution(14683996869458757858)
XLA Ops:
  0.6 0.0 copy-start.1
  0.6 0.0 copy-start.2
  0.7 0.0 copy-start.3
  0.7 1.7 %shard_map.67 = (f32[256,128]{1,0:T(8,128)S(1)}, f32[256,128]{1,0:T(8,128)S(1)}) custom-call(bf16[256,512]{1,0:T(8,128)(2,1)} %q_ref.3, bf16[256,512]{1,0:T(8,128)(2,1)} %k_ref.5, bf16[256,512]{1,0:T(8,128)(2,1)} %v_ref.5, bf16[256,512]{1,0:T(8,128)(2,1)} %d_ref.3), custom_call_target="tpu_custom_call" | custom-call | tf_op jit(solution)/shard_map/pallas_call | solution.py:254
  2.4 0.0 copy-start
  2.4 8.6 %all-gather = f32[512,128]{1,0:T(8,128)S(1)} all-gather(f32[256,128]{1,0:T(8,128)S(1)} %get-tuple-element.13), channel_id=2, replica_groups={{0,4},{8,12},{16,20},{24,28},{32,36},{40,44},{48,52},{56,60},{64,68},{7..., dimensions={0}, use_global_device_ids=true | all-gather | bytes 393216 | tf_op jit(solution)/shard_map/all_gather | solution.py:262
  11.0 0.0 copy-done.1
  11.0 0.0 copy-done.2
  11.0 0.0 copy-done.3
  11.0 0.0 copy-done
  11.0 1.8 %shard_map.68 = (f32[256,128]{1,0:T(8,128)S(1)}, f32[256,512]{1,0:T(8,128)S(1)}, f32[256,512]{1,0:T(8,128)S(1)}, f32[256,512]{1,0:T(8,128)S(1)}) custom-call(f32[256,128]{1,0:T(8,128)S(1)} %get-tuple-element.12.own_ref, f32[2,256,128]{2,1,0:T(8,128)S(1)} %bitcast.9, bf16[256,512]{1,0:T(8,128)(2,1)S(1)} %copy-done.2, bf16[256,512]{1,0:T(8,128)(2,1)S(1)} %copy-done, ...), custom_call_target="tpu_custom_call" | custom-call | tf_op jit(solution)/shard_map/pallas_call | solution.py:263
  12.9 15.6 %all_to_all.10 = f32[64,4,128]{2,1,0:T(4,128)S(1)} all-to-all(f32[64,4,128]{2,1,0:T(4,128)S(1)} %bitcast.12), channel_id=1, replica_groups={{288,296,304,312,320,328,336,344,352,360,368,376,384,392,400,408,416,42..., dimensions={0} | all-to-all | bytes 262144 | tf_op jit(solution)/shard_map/all_to_all | solution.py:269
  28.5 0.1 shard_map.69
  28.6 15.1 %all_to_all.11 = f32[64,4,128]{2,1,0:T(4,128)S(1)} all-to-all(f32[64,4,128]{2,1,0:T(4,128)S(1)} %bitcast.11), channel_id=1, replica_groups={{288,296,304,312,320,328,336,344,352,360,368,376,384,392,400,408,416,42..., dimensions={0} | all-to-all | bytes 262144 | tf_op jit(solution)/shard_map/all_to_all | solution.py:269
  43.6 0.3 shard_map.70
  44.0 3.3 %all-gather.1 = f32[512,128]{1,0:T(8,128)S(1)} all-gather(f32[256,128]{1,0:T(8,128)S(1)} %get-tuple-element.17), channel_id=3, replica_groups={{0,4},{8,12},{16,20},{24,28},{32,36},{40,44},{48,52},{56,60},{64,68},{7..., dimensions={0}, use_global_device_ids=true | all-gather | bytes 393216 | tf_op jit(solution)/shard_map/all_gather | solution.py:277
  47.3 1.0 %shard_map.71 = (bf16[256,512]{1,0:T(8,128)(2,1)}, bf16[256,512]{1,0:T(8,128)(2,1)}, bf16[256,512]{1,0:T(8,128)(2,1)}) custom-call(bf16[256,512]{1,0:T(8,128)(2,1)S(1)} %copy-done.2, bf16[256,512]{1,0:T(8,128)(2,1)S(1)} %copy-done, bf16[256,512]{1,0:T(8,128)(2,1)S(1)} %copy-done.1, bf16[256,512]{1,0:T(8,128)(2,1)S(1)} %copy-done.3, f32[256,128]{1,0:T(8,128)S(1)} %bitcast.7, ...), custom_call_target="tpu_custom_call" | custom-call | tf_op jit(solution)/shard_map/pallas_call | solution.py:278
Async XLA Ops:
  0.6 10.4 %copy-start.1 = (bf16[256,512]{1,0:T(8,128)(2,1)S(1)}, bf16[256,512]{1,0:T(8,128)(2,1)}, u32[]{:S(2)}) copy-start(bf16[256,512]{1,0:T(8,128)(2,1)} %v_ref.5) | copy-start | bytes 786436
  0.6 10.4 %copy-start.2 = (bf16[256,512]{1,0:T(8,128)(2,1)S(1)}, bf16[256,512]{1,0:T(8,128)(2,1)}, u32[]{:S(2)}) copy-start(bf16[256,512]{1,0:T(8,128)(2,1)} %q_ref.3) | copy-start | bytes 786436
  0.7 10.4 %copy-start.3 = (bf16[256,512]{1,0:T(8,128)(2,1)S(1)}, bf16[256,512]{1,0:T(8,128)(2,1)}, u32[]{:S(2)}) copy-start(bf16[256,512]{1,0:T(8,128)(2,1)} %d_ref.3) | copy-start | bytes 786436
  2.4 8.7 %copy-start = (bf16[256,512]{1,0:T(8,128)(2,1)S(1)}, bf16[256,512]{1,0:T(8,128)(2,1)}, u32[]{:S(2)}) copy-start(bf16[256,512]{1,0:T(8,128)(2,1)} %k_ref.5) | copy-start | bytes 786436
